TPU v7x, 32 devices: a whole 2x2x4 slice. The times are simulated.
32 devices in a mesh: up: 8 (over z, y), down: 4 (over x, core).
Axes of the slice: x: 2, y: 2, z: 4, core: 2. Of those that a mesh axis runs over, the one named last changes fastest.
Arguments:
- amplitudes: float32 [4096, 4096], P('up', 'down'), may hold values from -6 to 6
- double_occ: int32 [4096, 4096], P('up', 'down'), may hold values from 0 to 8
- up_cols: int32 [64, 32], replicated, may hold values from 0 to 63, as said below
- up_ids: int32 [64, 32], replicated, may hold values from 0 to 31, as said below
- up_blocks: bfloat16 [32, 64, 64], replicated, may hold values from -0.125 to 0.125
- down_cols: int32 [64, 32], replicated, may hold values from 0 to 63, as said below
- down_ids: int32 [64, 32], replicated, may hold values from 0 to 31, as said below
- down_blocks: bfloat16 [32, 64, 64], replicated, may hold values from -0.125 to 0.125
Outputs:
- chebyshev: float32 [4096, 4096], P('up', 'down')
Inputs may be any that keep to these rules, and one draw needn't show every extreme that they name: `up_cols`: each row names 32 different blocks. `up_ids`: each row names every shared block exactly once. `down_cols`: each row names 32 different blocks. `down_ids`: each row names every shared block exactly once.
All inputs are finite; a program needn't handle non-finite values.
Results may differ from a plain program's by a relative error of at most 0.0031.
Values may be sent and summed in bfloat16 or wider, within the bound.
A program may use at most 128 MiB of HBM per device.

v0:
```python
import math

import jax
import jax.numpy as jnp
from jax import lax
from jax.sharding import PartitionSpec as P

coupling = 0.5
center = 2.0
half_span = 2.0


def block_order(block_cols, block_ids, shared_count):
    matched = block_ids[:, :, None] == jnp.arange(shared_count, dtype=jnp.int32)[None, None, :]
    return jnp.sum(jnp.where(matched, block_cols[:, :, None], 0), axis=1)


def hop_strings(values, by_shared, shared_table):
    row_count = values.shape[0]
    shared_count = shared_table.shape[0]
    block_width = shared_table.shape[1]
    block_total = values.shape[1] // block_width
    out_blocks = by_shared.shape[0]
    pieces = values.reshape(row_count, block_total, block_width)
    flat_table = shared_table.reshape(shared_count * block_width, block_width)
    group_size = math.gcd(8, out_blocks)

    def one_group(step_index, result):
        chosen = lax.dynamic_slice_in_dim(
            by_shared, step_index * group_size, group_size, 0
        ).reshape(-1)
        taken_rows = jnp.take(pieces, chosen, axis=1).reshape(
            row_count * group_size, shared_count * block_width
        )
        block_out = jnp.dot(taken_rows, flat_table, preferred_element_type=jnp.float32)
        block_out = block_out.reshape(row_count, group_size * block_width)
        return lax.dynamic_update_slice_in_dim(
            result, block_out, step_index * group_size * block_width, 1
        )

    result = jnp.zeros((row_count, out_blocks * block_width), jnp.float32)
    return lax.fori_loop(0, out_blocks // group_size, one_group, result)


def body(amplitudes, double_occ, up_cols, up_ids, up_blocks, down_cols, down_ids, down_blocks):
    shared_count = up_blocks.shape[0]
    block_width = up_blocks.shape[1]
    local_rows, local_cols = amplitudes.shape
    up_count = lax.axis_size("up")
    up_order = block_order(up_cols, up_ids, shared_count)
    down_order = block_order(down_cols, down_ids, shared_count)
    onsite = coupling * double_occ.astype(jnp.float32) - center

    def apply_up(items):
        return hop_strings(items[0], up_order, up_blocks)[None]

    def up_part(rounded):
        sectioned = rounded.T.reshape(up_count, local_cols // up_count, local_rows)
        exchanged = apply_up(
            lax.all_to_all(sectioned, "up", split_axis=0, concat_axis=2, tiled=True)
        )
        returned = lax.all_to_all(exchanged, "up", split_axis=2, concat_axis=0, tiled=True)
        return returned.reshape(local_cols, local_rows).T

    def down_part(rounded):
        gathered = lax.all_gather(rounded, "down", axis=1, tiled=True)
        own_blocks = local_cols // block_width
        own_order = lax.dynamic_slice_in_dim(
            down_order, lax.axis_index("down") * own_blocks, own_blocks, 0
        )
        return hop_strings(gathered, own_order, down_blocks)

    def apply_scaled(current):
        rounded = current.astype(jnp.bfloat16)
        return (onsite * current + up_part(rounded) + down_part(rounded)) / half_span

    first = apply_scaled(amplitudes)
    return 2.0 * apply_scaled(first) - amplitudes


def solution(mesh):
    placed = (P("up", "down"), P("up", "down"), P(), P(), P(), P(), P(), P())
    return jax.shard_map(
        body, mesh=mesh, in_specs=placed, out_specs=P("up", "down"), check_vma=False
    )
```

profile of v0, /device:TPU:18, one launch (start us, length us, event | category | flops | bytes accessed | tf_op | source)
XLA Modules:
  0.0 1312.6 jit_solution(10178273621257362039)
XLA Ops:
  17.2 21.6 %all-to-all-done = bf16[8,128,512]{2,1,0:T(8,128)(2,1)S(1)} async-done(((bf16[8,128,512]{2,1,0:T(8,128)(2,1)}), bf16[8,128,512]{2,1,0:T(8,128)(2,1)S(1)}, u32[]{:S(2)}, u32[]{:S(2)}) %all-to-all-start) | async-done | bytes 1048608 | tf_op jit(solution)/shard_map/all_to_all | solution.py:60
  40.9 294.6 %while.60 = (s32[]{:T(128)}, f32[128,4096]{0,1:T(8,128)}, s32[64,32]{1,0:T(8,128)S(1)}, bf16[128,64,64]{0,2,1:T(8,128)(2,1)S(1)}, bf16[2048,64]{1,0:T(8,128)(2,1...) while((s32[]{:T(128)}, f32[128,4096]{0,1:T(8,128)}, ...), condition=%wide.region_2.4_spmd, body=%wide.region_1.0_spmd.sunk | while | flops 270535936 | bytes 39859920 | solution.py:42
  48.1 12.9 copy.131
  61.0 12.3 reshape.239
  85.0 12.9 copy.131
  97.8 12.3 reshape.239
  121.8 12.9 copy.131
  134.7 12.3 reshape.239
  158.7 12.9 copy.131
  171.5 12.3 reshape.239
  195.5 12.9 copy.131
  208.3 12.3 reshape.239
  232.3 12.9 copy.131
  245.2 12.3 reshape.239
  269.1 12.9 copy.131
  282.0 12.3 reshape.239
  305.9 12.9 copy.131
  318.8 12.3 reshape.239
  346.2 42.1 %all-to-all-done.1 = f32[1,128,4096]{1,0,2:T(1,128)S(1)} async-done(((f32[1,128,4096]{1,0,2:T(1,128)}), f32[1,128,4096]{1,0,2:T(1,128)S(1)}, u32[]{:S(2)}, u32[]{:S(2)}) %all-to-all-start.1) | async-done | bytes 2097184 | tf_op jit(solution)/shard_map/all_to_all | solution.py:62
  391.7 256.5 %while.61 = (s32[]{:T(128)}, f32[512,1024]{0,1:T(8,128)}, s32[16,32]{1,0:T(8,128)S(1)}, bf16[512,64,64]{0,2,1:T(8,128)(2,1)}, bf16[2048,64]{1,0:T(8,128)(2,1)S(1...) while((s32[]{:T(128)}, f32[512,1024]{0,1:T(8,128)}, ...), condition=%wide.region_5.8_spmd, body=%wide.region_4.7_spmd.sunk | while | flops 1082133760 | bytes 159659792 | solution.py:42
  403.9 14.2 %select_bitcast_fusion.9 = bf16[512,256,64]{0,2,1:T(8,128)(2,1)} fusion(bf16[256,512,64]{1,2,0:T(8,128)(2,1)} %gather_fusion.1, pred[256]{0:T(512)(128)(4,1)S(1)} %compare_and_fusion.9), kind=kLoop, calls=%fused_computation.10.clone.1 | loop fusion | flops 8388608 | bytes 33554688 | tf_op jit(solution)/shard_map/while/body/eval_jaxpr/jit(_take)/select_n | solution.py:32
  418.1 45.9 %copy.133 = bf16[512,256,64]{2,1,0:T(8,128)(2,1)} copy(bf16[512,256,64]{0,2,1:T(8,128)(2,1)} %select_bitcast_fusion.9) | data formatting | bytes 33554432 | tf_op jit(solution)/shard_map/while/body/eval_jaxpr/jit(_take)/select_n | solution.py:32
  464.0 45.9 %reshape.244 = bf16[4096,2048]{1,0:T(8,128)(2,1)} reshape(bf16[512,256,64]{2,1,0:T(8,128)(2,1)} %copy.133) | data formatting | bytes 33554432 | tf_op jit(solution)/shard_map/while/body/eval_jaxpr/reshape | solution.py:32
  532.2 14.2 %select_bitcast_fusion.9 = bf16[512,256,64]{0,2,1:T(8,128)(2,1)} fusion(bf16[256,512,64]{1,2,0:T(8,128)(2,1)} %gather_fusion.1, pred[256]{0:T(512)(128)(4,1)S(1)} %compare_and_fusion.9), kind=kLoop, calls=%fused_computation.10.clone.1 | loop fusion | flops 8388608 | bytes 33554688 | tf_op jit(solution)/shard_map/while/body/eval_jaxpr/jit(_take)/select_n | solution.py:32
  546.3 45.9 %copy.133 = bf16[512,256,64]{2,1,0:T(8,128)(2,1)} copy(bf16[512,256,64]{0,2,1:T(8,128)(2,1)} %select_bitcast_fusion.9) | data formatting | bytes 33554432 | tf_op jit(solution)/shard_map/while/body/eval_jaxpr/jit(_take)/select_n | solution.py:32
  592.3 45.9 %reshape.244 = bf16[4096,2048]{1,0:T(8,128)(2,1)} reshape(bf16[512,256,64]{2,1,0:T(8,128)(2,1)} %copy.133) | data formatting | bytes 33554432 | tf_op jit(solution)/shard_map/while/body/eval_jaxpr/reshape | solution.py:32
  661.4 21.9 %all-to-all-done.2 = bf16[8,128,512]{2,1,0:T(8,128)(2,1)S(1)} async-done(((bf16[8,128,512]{2,1,0:T(8,128)(2,1)}), bf16[8,128,512]{2,1,0:T(8,128)(2,1)S(1)}, u32[]{:S(2)}, u32[]{:S(2)}) %all-to-all-start.2) | async-done | bytes 1048608 | tf_op jit(solution)/shard_map/all_to_all | solution.py:60
  685.5 300.0 %while.62 = (s32[]{:T(128)}, f32[128,4096]{0,1:T(8,128)}, s32[64,32]{1,0:T(8,128)}, bf16[128,64,64]{0,2,1:T(8,128)(2,1)S(1)}, bf16[2048,64]{1,0:T(8,128)(2,1)S(1...) while((s32[]{:T(128)}, f32[128,4096]{0,1:T(8,128)}, ...), condition=%wide.region_7.10_spmd, body=%wide.region_6.0_spmd.sunk | while | flops 270535936 | bytes 39859920 | solution.py:42
  693.3 12.9 copy.135
  706.2 12.3 reshape.249
  730.8 12.9 copy.135
  743.7 12.3 reshape.249
  768.3 12.9 copy.135
  781.2 12.3 reshape.249
  805.9 12.9 copy.135
  818.7 12.3 reshape.249
  843.3 12.9 copy.135
  880.9 12.9 copy.135
  918.4 12.9 copy.135
  955.9 12.9 copy.135
  992.4 45.2 %all-to-all-done.3 = f32[1,128,4096]{1,0,2:T(1,128)S(1)} async-done(((f32[1,128,4096]{1,0,2:T(1,128)}), f32[1,128,4096]{1,0,2:T(1,128)S(1)}, u32[]{:S(2)}, u32[]{:S(2)}) %all-to-all-start.3) | async-done | bytes 2097184 | tf_op jit(solution)/shard_map/all_to_all | solution.py:62
  1041.1 256.6 %while.63 = (s32[]{:T(128)}, f32[512,1024]{0,1:T(8,128)}, s32[16,32]{1,0:T(8,128)S(1)}, bf16[512,64,64]{0,2,1:T(8,128)(2,1)}, bf16[2048,64]{1,0:T(8,128)(2,1)}, ...) while((s32[]{:T(128)}, f32[512,1024]{0,1:T(8,128)}, ...), condition=%wide.region_9.12_spmd, body=%wide.region_8.11_spmd.sunk | while | flops 1082133760 | bytes 158611184 | solution.py:42
  1053.2 14.2 %select_bitcast_fusion.11 = bf16[512,256,64]{0,2,1:T(8,128)(2,1)} fusion(bf16[256,512,64]{1,2,0:T(8,128)(2,1)} %gather_fusion.3, pred[256]{0:T(512)(128)(4,1)S(1)} %compare_and_fusion.11), kind=kLoop, calls=%fused_computation.22.clone.1 | loop fusion | flops 8388608 | bytes 33554688 | tf_op jit(solution)/shard_map/while/body/eval_jaxpr/jit(_take)/select_n | solution.py:32
  1067.4 45.9 %copy.137 = bf16[512,256,64]{2,1,0:T(8,128)(2,1)} copy(bf16[512,256,64]{0,2,1:T(8,128)(2,1)} %select_bitcast_fusion.11) | data formatting | bytes 33554432 | tf_op jit(solution)/shard_map/while/body/eval_jaxpr/jit(_take)/select_n | solution.py:32
  1113.4 45.9 %reshape.254 = bf16[4096,2048]{1,0:T(8,128)(2,1)} reshape(bf16[512,256,64]{2,1,0:T(8,128)(2,1)} %copy.137) | data formatting | bytes 33554432 | tf_op jit(solution)/shard_map/while/body/eval_jaxpr/reshape | solution.py:32
  1181.5 14.2 %select_bitcast_fusion.11 = bf16[512,256,64]{0,2,1:T(8,128)(2,1)} fusion(bf16[256,512,64]{1,2,0:T(8,128)(2,1)} %gather_fusion.3, pred[256]{0:T(512)(128)(4,1)S(1)} %compare_and_fusion.11), kind=kLoop, calls=%fused_computation.22.clone.1 | loop fusion | flops 8388608 | bytes 33554688 | tf_op jit(solution)/shard_map/while/body/eval_jaxpr/jit(_take)/select_n | solution.py:32
  1195.7 45.9 %copy.137 = bf16[512,256,64]{2,1,0:T(8,128)(2,1)} copy(bf16[512,256,64]{0,2,1:T(8,128)(2,1)} %select_bitcast_fusion.11) | data formatting | bytes 33554432 | tf_op jit(solution)/shard_map/while/body/eval_jaxpr/jit(_take)/select_n | solution.py:32
  1241.6 45.9 %reshape.254 = bf16[4096,2048]{1,0:T(8,128)(2,1)} reshape(bf16[512,256,64]{2,1,0:T(8,128)(2,1)} %copy.137) | data formatting | bytes 33554432 | tf_op jit(solution)/shard_map/while/body/eval_jaxpr/reshape | solution.py:32
  (271 shorter events, 390.0 us)
Async XLA Ops:
  8.5 1.7 copy-start.2
  9.7 7.3 copy-start.4
  9.7 7.3 copy-start.5
  10.1 28.7 %all-to-all-start = ((bf16[8,128,512]{2,1,0:T(8,128)(2,1)}), bf16[8,128,512]{2,1,0:T(8,128)(2,1)S(1)}, u32[]{:S(2)}, u32[]{:S(2)}) async-start(bf16[8,128,512]{2,1,0:T(8,128)(2,1)} %bitcast.5), calls=%async_computation | async-start | bytes 2097152 | tf_op jit(solution)/shard_map/all_to_all | solution.py:60
  16.3 373.9 %all-gather.3.cloned.1.call-start = ((), (), s32[]{:S(2)}) async-start(), calls=%async_computation.4 | async-start | bytes 5242880 | tf_op jit(solution)/shard_map/all_gather | solution.py:66
  38.8 2.1 copy-start
  335.6 0.6 copy-start.3
  335.6 7.5 copy-start.6
  335.6 7.5 copy-start.7
  336.2 52.1 %all-to-all-start.1 = ((f32[1,128,4096]{1,0,2:T(1,128)}), f32[1,128,4096]{1,0,2:T(1,128)S(1)}, u32[]{:S(2)}, u32[]{:S(2)}) async-start(f32[1,128,4096]{1,0,2:T(1,128)} %bitcast.94), calls=%async_computation.1 | async-start | bytes 4194304 | tf_op jit(solution)/shard_map/all_to_all | solution.py:62
  390.1 1.6 copy-start.8
  518.9 1.2 copy-start.9
  647.1 1.2 copy-start.9
  653.8 29.5 %all-to-all-start.2 = ((bf16[8,128,512]{2,1,0:T(8,128)(2,1)}), bf16[8,128,512]{2,1,0:T(8,128)(2,1)S(1)}, u32[]{:S(2)}, u32[]{:S(2)}) async-start(bf16[8,128,512]{2,1,0:T(8,128)(2,1)} %bitcast.18), calls=%async_computation.2 | async-start | bytes 2097152 | tf_op jit(solution)/shard_map/all_to_all | solution.py:60
  660.6 378.9 %all-gather.5.cloned.1.call-start = ((), (), s32[]{:S(2)}) async-start(), calls=%async_computation.5 | async-start | bytes 5242880 | tf_op jit(solution)/shard_map/all_gather | solution.py:66
  683.3 2.2 copy-start.1
  985.5 52.2 %all-to-all-start.3 = ((f32[1,128,4096]{1,0,2:T(1,128)}), f32[1,128,4096]{1,0,2:T(1,128)S(1)}, u32[]{:S(2)}, u32[]{:S(2)}) async-start(f32[1,128,4096]{1,0,2:T(1,128)} %bitcast.95), calls=%async_computation.3 | async-start | bytes 4194304 | tf_op jit(solution)/shard_map/all_to_all | solution.py:62
Sparse Core Ops, SparseCore 0:
  18.7 34.4 all-gather.2
  663.0 34.4 all-gather.4
where the time goes:
time: 1340 us; the launch traced here: 1310 us
  local copies, waits for them, and re-layouts  917 us (68%)
  other arithmetic  135 us (10%)
  waiting for transfers between devices  132 us (10%)
  matrix products  87.7 us (7%)
  starting transfers between devices  26.8 us (2%)
  between operations  13.5 us (1%)
    select_n x20, local copies, waits for them, and re-layouts, one_group(): jnp.take(pieces, chosen, axis=1)  389 us
    reshape x20, local copies, waits for them, and re-layouts, one_group(): jnp.take(pieces, chosen, axis=1)  381 us
    select_n x40, other arithmetic, one_group(): jnp.take(pieces, chosen, axis=1)  121 us
    gather x20, local copies, waits for them, and re-layouts, one_group(): jnp.take(pieces, chosen, axis=1)  97.2 us
    dot_general x20, matrix products, one_group(): jnp.dot(taken_rows, flat_table, preferred_element_type=jnp.float32)  87.7 us
    all_to_all x2, waiting for transfers between devices, up_part(): lax.all_to_all(exchanged, 'up', split_axis=2, concat_axis=0, tiled=True)  87.3 us
    all_to_all x2, waiting for transfers between devices, up_part(): lax.all_to_all(sectioned, 'up', split_axis=0, concat_axis=2, tiled=True)  43.5 us
  transfers between devices with their start and end apart: 6, of which 4 were waited for; matrix products, arithmetic and copies ran while one was open for 46% of the time, Pallas kernels for 0%

commit v1 on v0

v1 whole, which is shorter than its diff:
```python
import functools
import math

import jax
import jax.numpy as jnp
from jax import lax
from jax.experimental import pallas as pl
from jax.experimental.pallas import tpu as pltpu
from jax.sharding import PartitionSpec as P

coupling = 0.5
center = 2.0
LANES = 128
MESH = pl.DeviceIdType.MESH
F32 = jnp.float32
BF16 = jnp.bfloat16


def kernel(dims, up_map, down_map, amp, occ, up_tab, down_tab, out,
           tup, tdn, gath, vbuf, ret_out, ret_in, dsum, first,
           zs, zr, ys, yr, rs, rr, xs, xr, cs, cr):
    A, B, X, C, R, blk = dims
    DN = 2 * X
    u = lax.axis_index("up")
    d = lax.axis_index("down")
    me_a, me_b = lax.div(u, B), lax.rem(u, B)
    me_x, me_k = lax.div(d, 2), lax.rem(d, 2)
    AW = A * LANES
    sends = []

    def at_a(da):
        return lax.rem(me_a + da + A, A)

    def at_b(db):
        return lax.rem(me_b + db + B, B)

    def at_x(dx):
        return lax.rem(me_x + dx + X, X)

    def start(src, dst, ssem, rsem, dev):
        copy = pltpu.make_async_remote_copy(
            src_ref=src, dst_ref=dst, send_sem=ssem, recv_sem=rsem,
            device_id=dev, device_id_type=MESH)
        copy.start()
        sends.append(copy)

    def arrived(ref, ssem, rsem, dev):
        pltpu.make_async_remote_copy(
            src_ref=ref, dst_ref=ref, send_sem=ssem, recv_sem=rsem,
            device_id=dev, device_id_type=MESH).wait_recv()

    def forward_y(s, c, da):
        piece = vbuf.at[s, c, at_a(-da), me_b]
        for db in range(1, B):
            start(piece, piece, ys.at[s, c, da, db], yr.at[s, c, da, db],
                  (me_a * B + at_b(db), d))

    def forward_core(s, c, dx):
        piece = gath.at[s, at_x(-dx) * 2 + me_k, c]
        start(piece, piece, cs.at[s, c, dx], cr.at[s, c, dx], (u, me_x * 2 + 1 - me_k))

    def send_z(s, c):
        for da in z_order:
            start(gath.at[s, d, c, at_a(da)], vbuf.at[s, c, me_a, me_b],
                  zs.at[s, c, da], zr.at[s, c, da], (at_a(da) * B + me_b, d))
        vbuf[s, c, me_a, me_b] = gath[s, d, c, me_a]
        forward_y(s, c, 0)

    def send_down(s, c):
        for dx in range(1, X):
            piece = gath.at[s, d, c]
            start(piece, piece, xs.at[s, c, dx], xr.at[s, c, dx], (u, at_x(dx) * 2 + me_k))
        forward_core(s, c, 0)

    def take_z(s, c):
        for da in range(1, A):
            arrived(vbuf.at[s, c, at_a(-da), me_b], zs.at[s, c, da], zr.at[s, c, da],
                    (at_a(-da) * B + me_b, d))
            forward_y(s, c, da)

    def take_x(s, c):
        for dx in range(1, X):
            arrived(gath.at[s, at_x(-dx) * 2 + me_k, c], xs.at[s, c, dx], xr.at[s, c, dx],
                    (u, at_x(-dx) * 2 + me_k))
            forward_core(s, c, dx)

    def take_y(s, c):
        for da in range(A):
            for db in range(1, B):
                arrived(vbuf.at[s, c, at_a(-da), at_b(-db)], ys.at[s, c, da, db],
                        yr.at[s, c, da, db], (me_a * B + at_b(-db), d))

    def take_core(s, c):
        for dx in range(X):
            arrived(gath.at[s, at_x(-dx) * 2 + 1 - me_k, c], cs.at[s, c, dx], cr.at[s, c, dx],
                    (u, me_x * 2 + 1 - me_k))

    z_order = [A // 2] + [da for da in range(1, A) if da != A // 2]
    step_rows = math.gcd(R, 256)

    def up_hop(s, c):
        for da in z_order + [0]:
            dest = at_a(da)
            put = ret_in.at[s, c, me_a] if da == 0 else ret_out.at[s, c, da]

            def rows(i, _):
                base = pl.multiple_of(i * step_rows, step_rows)
                left = tup[dest, pl.ds(base, step_rows), :]
                right = vbuf[s, c].reshape(A * B * R, LANES)
                put[pl.ds(base, step_rows), :] = jnp.dot(
                    left, right, preferred_element_type=F32).astype(BF16)
                return 0

            lax.fori_loop(0, R // step_rows, rows, 0)
            if da:
                start(put, ret_in.at[s, c, me_a], rs.at[s, c, da], rr.at[s, c, da],
                      (dest * B + me_b, d))

    def take_ret(s, c):
        for da in range(1, A):
            arrived(ret_in.at[s, c, at_a(-da)], rs.at[s, c, da], rr.at[s, c, da],
                    (at_a(-da) * B + me_b, d))

    def down_hop(s):
        dsum[...] = jnp.zeros_like(dsum)
        per_n = 256
        for c in range(C):
            def part(i, _):
                src = lax.div(i, C * AW // per_n)
                col = pl.multiple_of(lax.rem(i, C * AW // per_n) * per_n, per_n)
                left = jnp.concatenate([gath[s, src, c, a] for a in range(A)], axis=1)
                k0 = pl.multiple_of((src * C + c) * AW, AW)
                dsum[:, pl.ds(col, per_n)] += jnp.dot(
                    left, tdn[pl.ds(k0, AW), pl.ds(col, per_n)], preferred_element_type=F32)
                return 0

            lax.fori_loop(0, DN * (C * AW // per_n), part, 0)

    def tiles(c, work):
        def one(i, _):
            base = pl.multiple_of(i * tile_rows, tile_rows)
            rows = pl.ds(base, tile_rows)
            for a in range(A):
                work(a, rows, pl.ds((a * C + c) * LANES, LANES), pl.ds(c * AW + a * LANES, LANES))
            return 0

        tile_rows = math.gcd(R, 64)
        lax.fori_loop(0, R // tile_rows, one, 0)

    def round_in(c):
        def work(a, rows, cols, inner):
            gath[0, d, c, a, rows, :] = amp[rows, cols].astype(BF16)
        tiles(c, work)

    def combine(c):
        def work(a, rows, cols, inner):
            onsite = coupling * occ[rows, cols].astype(F32) - center
            value = (onsite * amp[rows, cols] + ret_in[0, c, a, rows, :].astype(F32)
                     + dsum[rows, inner]) * 0.5
            first[rows, inner] = value
            gath[1, d, c, a, rows, :] = value.astype(BF16)
        tiles(c, work)

    def finish(c):
        def work(a, rows, cols, inner):
            onsite = coupling * occ[rows, cols].astype(F32) - center
            out[rows, cols] = (onsite * first[rows, inner] + ret_in[1, c, a, rows, :].astype(F32)
                               + dsum[rows, inner]) - amp[rows, cols]
        tiles(c, work)

    per_dev = R // blk

    def build_up():
        def one(i, _):
            a, rb = lax.div(i, per_dev), lax.rem(i, per_dev)
            row = (a * B + me_b) * per_dev + rb
            r0 = pl.multiple_of(rb * blk, blk)
            for j in range(A * B * R // LANES):
                tup[a, pl.ds(r0, blk), pl.ds(j * LANES, LANES)] = (
                    up_tab[0, up_map[row, 2 * j]] + up_tab[1, up_map[row, 2 * j + 1]])
            return 0
        lax.fori_loop(0, A * per_dev, one, 0)

    def build_down():
        two = LANES // blk

        def one(i, _):
            blocks = C * A
            src, rest = lax.div(i, blocks), lax.rem(i, blocks)
            c, a = lax.div(rest, A), lax.rem(rest, A)
            for h in range(two):
                col_block = (src * blocks + a * C + c) * two + h
                r0 = pl.multiple_of(i * LANES + h * blk, blk)
                for n in range(blocks):
                    nc, na = n // A, n % A
                    out_block = (d * blocks + na * C + nc) * two
                    tdn[pl.ds(r0, blk), pl.ds(n * LANES, LANES)] = (
                        down_tab[0, down_map[out_block, col_block]]
                        + down_tab[1, down_map[out_block + 1, col_block]])
            return 0
        lax.fori_loop(0, DN * C * A, one, 0)

    barrier = pltpu.get_barrier_semaphore()
    partners = ([(at_a(da) * B + me_b, d) for da in range(1, A)]
                + [(me_a * B + at_b(db), d) for db in range(1, B)]
                + [(u, at_x(dx) * 2 + me_k) for dx in range(1, X)]
                + [(u, me_x * 2 + 1 - me_k)])
    for dev in partners:
        pl.semaphore_signal(barrier, inc=1, device_id=dev, device_id_type=MESH)
    round_in(0)
    pl.semaphore_wait(barrier, len(partners))

    for c in range(C):
        if c:
            round_in(c)
        send_z(0, c)
        send_down(0, c)
    build_up()
    take_z(0, 0)
    take_x(0, 0)
    build_down()
    for c in range(C):
        if c:
            take_z(0, c)
            take_x(0, c)
        take_y(0, c)
        up_hop(0, c)
    for c in range(C):
        take_core(0, c)
    down_hop(0)
    for c in range(C):
        take_ret(0, c)
        combine(c)
        send_z(1, c)
        send_down(1, c)
    for c in range(C):
        take_z(1, c)
        take_x(1, c)
        take_y(1, c)
        up_hop(1, c)
    for c in range(C):
        take_core(1, c)
    down_hop(1)
    for c in range(C):
        take_ret(1, c)
        finish(c)
    for copy in sends:
        copy.wait_send()


def body(up_count, down_count, amplitudes, double_occ, up_cols, up_ids, up_blocks,
         down_cols, down_ids, down_blocks):
    R, W = amplitudes.shape
    shared, blk = up_blocks.shape[:2]
    total = up_cols.shape[0]
    A = math.gcd(4, up_count)
    B = up_count // A
    X = down_count // 2
    C = W // (A * LANES)

    def block_map(cols, ids):
        hit = cols[:, :, None] == jnp.arange(total, dtype=jnp.int32)[None, None, :]
        return jnp.sum(jnp.where(hit, ids[:, :, None] + 1, 0), axis=1)

    def table(blocks):
        low = jnp.pad(blocks, ((1, 0), (0, 0), (0, LANES - blk)))
        high = jnp.pad(blocks, ((1, 0), (0, 0), (LANES - blk, 0)))
        return jnp.stack([low, high])

    vmem = pl.BlockSpec(memory_space=pltpu.VMEM)
    smem = pl.BlockSpec(memory_space=pltpu.SMEM)
    dma = pltpu.SemaphoreType.DMA
    return pl.pallas_call(
        functools.partial(kernel, (A, B, X, C, R, blk)),
        out_shape=jax.ShapeDtypeStruct((R, W), F32),
        in_specs=[smem, smem, vmem, vmem, vmem, vmem],
        out_specs=vmem,
        scratch_shapes=[
            pltpu.VMEM((A, R, total * blk), BF16),
            pltpu.VMEM((total * blk, W), BF16),
            pltpu.VMEM((2, down_count, C, A, R, LANES), BF16),
            pltpu.VMEM((2, C, A, B, R, LANES), BF16),
            pltpu.VMEM((2, C, A, R, LANES), BF16),
            pltpu.VMEM((2, C, A, R, LANES), BF16),
            pltpu.VMEM((R, W), F32),
            pltpu.VMEM((R, W), F32),
            dma((2, C, A)), dma((2, C, A)),
            dma((2, C, A, B)), dma((2, C, A, B)),
            dma((2, C, A)), dma((2, C, A)),
            dma((2, C, X)), dma((2, C, X)),
            dma((2, C, X)), dma((2, C, X)),
        ],
        compiler_params=pltpu.CompilerParams(
            collective_id=0, has_side_effects=True, vmem_limit_bytes=60 * 2**20),
    )(block_map(up_cols, up_ids), block_map(down_cols, down_ids), amplitudes, double_occ,
      table(jnp.swapaxes(up_blocks, 1, 2)), table(down_blocks))


def solution(mesh):
    placed = (P("up", "down"), P("up", "down"), P(), P(), P(), P(), P(), P())
    return jax.shard_map(
        functools.partial(body, mesh.shape["up"], mesh.shape["down"]),
        mesh=mesh, in_specs=placed, out_specs=P("up", "down"), check_vma=False)
```

time: 1340 us -> 128 us (0.10); the launches traced: 1310 us -> 128 us
  local copies, waits for them, and re-layouts: 917 us -> 5.5 us
  waiting for transfers between devices: 132 us -> 0 us
  other arithmetic: 135 us -> 3.59 us
  Pallas kernels: 0 us -> 119 us
  matrix products: 87.7 us -> 0 us
  starting transfers between devices: 26.8 us -> 0 us
  between operations: 13.5 us -> 0.09 us
    select_n x20 -> x0, local copies, waits for them, and re-layouts: 389 us -> none  [one_group(): jnp.take(pieces, chosen, axis=1)]
    reshape x60 -> x0, local copies, waits for them, and re-layouts: 387 us -> none  [the longest x20 381 us: one_group(): jnp.take(pieces, chosen, axis=1)]
    all_to_all x4 -> x0, waiting for transfers between devices: 131 us -> none  [the longest x2 87.3 us: up_part(): lax.all_to_all(exchanged, 'up', split_axis=2, concat_axis=0, tiled=True)]
    select_n x40 -> x0, other arithmetic: 121 us -> none  [one_group(): jnp.take(pieces, chosen, axis=1)]
    pallas_call x0 -> x1, Pallas kernels: none -> 119 us  [body(): pl.pallas_call(functools.partial(kernel, (A, B, X, C, R, blk)), out_shape...]
    gather x20 -> x0, local copies, waits for them, and re-layouts: 97.2 us -> none  [one_group(): jnp.take(pieces, chosen, axis=1)]
    dot_general x20 -> x0, matrix products: 87.7 us -> none  [one_group(): jnp.dot(taken_rows, flat_table, preferred_element_type=jnp.float32)]
    all_to_all x4 -> x0, starting transfers between devices: 26.8 us -> none  [the longest x2 13.8 us: up_part(): lax.all_to_all(exchanged, 'up', split_axis=2, concat_axis=0, tiled=True)]
  transfers between devices with their start and end apart: 6 -> 0, of which waited for: 4 -> 0; matrix products, arithmetic and copies ran while one was open for 46% -> 0% of each run, Pallas kernels for 0% -> 0%
where the time goes in v1:
time: 128 us
  Pallas kernels  119 us (93%)
  local copies, waits for them, and re-layouts  5.5 us (4%)
  other arithmetic  3.59 us (3%)
    pallas_call x1, Pallas kernels, body(): pl.pallas_call(functools.partial(kernel, (A, B, X, C, R, blk)), out_shape...  119 us
    unnamed x14, local copies, waits for them, and re-layouts  4.71 us

profile of v1, /device:TPU:18, one launch (start us, length us, event | category | flops | bytes accessed | tf_op | source)
XLA Modules:
  0.0 127.8 jit_solution(10683069180296041995)
XLA Ops:
  0.0 0.0 copy-start
  0.0 1.4 %copy.18 = bf16[32,64,64]{1,2,0:T(8,128)(2,1)S(1)} copy(bf16[32,64,64]{2,1,0:T(8,128)(2,1)} %param.12) | data formatting | bytes 524288 | tf_op args[4]
  1.4 0.3 pad_bitcast_fusion.3
  1.7 0.0 copy-done
  1.7 0.3 pad_bitcast_fusion.1
  2.0 0.0 copy-start.3
  2.0 0.0 copy-start.4
  2.0 0.0 copy-start.1
  2.1 0.0 copy-start.2
  2.1 1.5 %pad_maximum_fusion = (bf16[2,33,64,128]{3,2,1,0:T(8,128)(2,1)}, bf16[2,33,64,128]{3,2,1,0:T(8,128)(2,1)}) fusion(bf16[1,33,64,128]{3,2,1,0:T(8,128)(2,1)S(1)} %get-tuple-element.8, bf16[1,33,64,128]{3,2,1,0:T(8,128)(2,1)S(1)} %get-tuple-element.7, bf16[1,33,64,128]{3,2,1,0:T(8,128)(2,1)S(1)} %get-tuple-element.6, bf16[1,33,64,128]{3,2,1,0:T(8,128)(2,1)S(1)} %get-tuple-element.5), kind=kLoop, calls=%fused_computation | loop fusion | flops 1081344 | bytes 4325376 | tf_op jit(solution)/shard_map/stack | solution.py:268
  3.6 0.0 copy-done.3
  3.6 0.1 copy.15
  3.7 0.0 copy-done.4
  3.7 0.1 copy.17
  3.8 0.0 copy-done.1
  3.8 0.1 copy.14
  3.9 0.0 copy-done.2
  3.9 0.1 copy.16
  4.0 2.0 %select_reduce_fusion = (s32[64,64]{1,0:T(8,128)}, s32[64,64]{1,0:T(8,128)}) fusion(s32[64,32]{1,0:T(8,128)S(1)} %copy.17, s32[64,32]{1,0:T(8,128)S(1)} %copy.16, s32[64,32]{1,0:T(8,128)S(1)} %copy.15, s32[64,32]{1,0:T(8,128)S(1)} %copy.14), kind=kLoop, calls=%fused_computation.2 | loop fusion | flops 778240 | bytes 65536 | tf_op jit(solution)/shard_map/reduce_sum | solution.py:263
  6.0 118.6 %shard_map.82 = f32[512,1024]{1,0:T(8,128)} custom-call(s32[64,64]{1,0:T(8,128)} %get-tuple-element.12.up_map, s32[64,64]{1,0:T(8,128)} %get-tuple-element.11.down_map, f32[512,1024]{1,0:T(8,128)} %amp.1, s32[512,1024]{1,0:T(8,128)} %occ.1, bf16[2,33,64,128]{3,2,1,0:T(8,128)(2,1)} %get-tuple-element.9.up_tab, bf16[2,33,64,128]{3,2,1,0:T(8,128)(2,1)} %get-tuple-element.10.down_tab), custom_call_target="tpu_custom_call" | custom-call | tf_op jit(solution)/shard_map/pallas_call | solution.py:273
  124.6 3.2 %copy.20 = f32[512,1024]{1,0:T(8,128)} copy(f32[512,1024]{1,0:T(8,128)} %shard_map.82) | data formatting | bytes 4194304
  (2 shorter events, 0.0 us)
Async XLA Ops:
  0.0 1.7 %copy-start = (bf16[32,64,64]{2,1,0:T(8,128)(2,1)S(1)}, bf16[32,64,64]{2,1,0:T(8,128)(2,1)}, u32[]{:S(2)}) copy-start(bf16[32,64,64]{2,1,0:T(8,128)(2,1)} %param.15) | copy-start | bytes 786436
  2.0 1.6 %copy-start.3 = (s32[64,32]{0,1:T(8,128)S(1)}, s32[64,32]{0,1:T(8,128)}, u32[]{:S(2)}) copy-start(s32[64,32]{0,1:T(8,128)} %param.11) | copy-start | bytes 24580
  2.0 1.7 %copy-start.4 = (s32[64,32]{0,1:T(8,128)S(1)}, s32[64,32]{0,1:T(8,128)}, u32[]{:S(2)}) copy-start(s32[64,32]{0,1:T(8,128)} %param.14) | copy-start | bytes 24580
  2.0 1.8 %copy-start.1 = (s32[64,32]{0,1:T(8,128)S(1)}, s32[64,32]{0,1:T(8,128)}, u32[]{:S(2)}) copy-start(s32[64,32]{0,1:T(8,128)} %param.10) | copy-start | bytes 24580
  2.1 1.8 %copy-start.2 = (s32[64,32]{0,1:T(8,128)S(1)}, s32[64,32]{0,1:T(8,128)}, u32[]{:S(2)}) copy-start(s32[64,32]{0,1:T(8,128)} %param.13) | copy-start | bytes 24580
